TPU v7x, 512 devices: a whole 4x4x16 slice. The times are simulated.
512 devices in a mesh: rows: 64 (over z, x), dims: 8 (over y, core).
Axes of the slice: x: 4, y: 4, z: 16, core: 2. Of those that a mesh axis runs over, the one named last changes fastest.
Arguments:
- noise_latents: bfloat16 [8192, 32768], P('rows', 'dims'), may hold values from -6 to 6
- data_latents: bfloat16 [1536, 32768], P('rows', 'dims'), may hold values from -6 to 6
Outputs:
- targets: bfloat16 [8192, 32768], P('rows', 'dims')
- column_potential: float32 [1536], replicated
All inputs are finite; a program needn't handle non-finite values.
Results may differ from a plain program's by a relative error of at most 0.0054.
Values may be sent and summed in bfloat16 or wider, within the bound.
A program may use at most 64 MiB of HBM per device.

v0:
```python
import math

import jax
import jax.numpy as jnp
from jax import lax
from jax.sharding import PartitionSpec as P

D = 32768
ITERS = 3


def row_logsumexp(scores):
    highest = jnp.max(scores, axis=1)
    totals = jnp.sum(jnp.exp(scores - highest[:, None]), axis=1)
    return highest + jnp.log(totals)


def column_logsumexp(scores):
    highest = jnp.max(scores, axis=0)
    highest = lax.pmax(highest, "rows")
    totals = lax.psum(jnp.sum(jnp.exp(scores - highest[None, :]), axis=0), "rows")
    return highest + jnp.log(totals)


def on_device(noise_latents, data_latents):
    entropic = 0.4 / math.sqrt(D)
    gathered = lax.all_gather(data_latents, "rows", axis=0, tiled=True)
    columns = gathered.shape[0]
    noise_total = noise_latents.shape[0] * lax.axis_size("rows")
    noise_sq = jnp.einsum(
        "id,id->i", noise_latents, noise_latents, preferred_element_type=jnp.float32
    )
    data_sq = jnp.einsum("jd,jd->j", gathered, gathered, preferred_element_type=jnp.float32)
    products = lax.dot_general(
        noise_latents, gathered, (((1,), (1,)), ((), ())), preferred_element_type=jnp.float32
    )
    partial_value = (noise_sq[:, None] + data_sq[None, :] - 2.0 * products) / D
    transport = lax.psum(partial_value, "dims")
    log_columns = jnp.log(jnp.float32(columns))
    log_rows = jnp.log(jnp.float32(noise_total))
    potential = jnp.zeros((transport.shape[1],), jnp.float32)
    for iteration in range(ITERS):
        row_potential = -entropic * (
            row_logsumexp((potential[None, :] - transport) / entropic) - log_columns
        )
        potential = -entropic * (
            column_logsumexp((row_potential[:, None] - transport) / entropic) - log_rows
        )
    scores = (potential[None, :] - transport) / entropic
    weights = jnp.exp(scores - row_logsumexp(scores)[:, None]).astype(jnp.bfloat16)
    targets = jnp.dot(weights, gathered, preferred_element_type=jnp.float32).astype(jnp.bfloat16)
    return (targets, potential)


def solution(mesh):
    placed = (P("rows", "dims"), P("rows", "dims"))
    return jax.shard_map(
        on_device, mesh=mesh, in_specs=placed, out_specs=(P("rows", "dims"), P()), check_vma=False
    )
```

profile of v0, /device:TPU:2, one launch (start us, length us, event | category | flops | bytes accessed | tf_op | source)
XLA Modules:
  0.0 1159.8 jit_solution(11294951632236456786)
XLA Ops:
  7.2 0.0 copy-start
  7.2 0.0 all-gather.2.cloned.1.call-start
  7.2 0.7 all-gather.2.cloned.1.call-update
  7.9 0.0 all-reduce.2.cloned.1.call-start
  8.0 1.5 fusion.3
  9.5 175.7 %all-gather.2.cloned.1.call-done = bf16[1536,4096]{1,0:T(8,128)(2,1)} async-done(((bf16[24,4096]{1,0:T(8,128)(2,1)}), bf16[1536,4096]{1,0:T(8,128)(2,1)}) %all-gather.2.cloned.1.call-update) | async-done | bytes 12582928 | tf_op jit(solution)/shard_map/all_gather | solution.py:27
  185.2 7.1 fusion
  192.2 0.0 copy-done
  192.2 9.7 fusion.2
  201.9 0.0 all-reduce.2.cloned.1.call-update
  201.9 73.5 %all-reduce.2.cloned.1.call-done = f32[128,1536]{1,0:T(8,128)} async-done(((f32[128,1536]{1,0:T(8,128)}), f32[128,1536]{1,0:T(8,128)}) %all-reduce.2.cloned.1.call-update) | async-done | bytes 786448 | tf_op jit(solution)/shard_map/psum | solution.py:38
  275.4 1.3 fusion.4
  276.7 1.4 exponential_reduce_fusion.6
  278.1 1.3 fusion.5
  279.4 142.2 %pmax.21 = f32[1536]{0:T(1024)S(1)} all-reduce(f32[1536]{0:T(1024)S(1)} %fusion.5), channel_id=1, replica_groups=mesh['rows'=64,'dims'=8] {'rows'}, use_global_device_ids=true, to_apply=%region_4.0 | all-reduce | flops 1536 | bytes 12288 | tf_op jit(solution)/shard_map/pmax | solution.py:20
  421.7 1.4 exponential_reduce_fusion.5
  423.0 144.5 %psum.29 = f32[1536]{0:T(1024)S(1)} all-reduce(f32[1536]{0:T(1024)S(1)} %exponential_reduce_fusion.5), channel_id=1, replica_groups=mesh['rows'=64,'dims'=8] {'rows'}, use_global_device_ids=true, to_apply=%region_6.0 | all-reduce | flops 1536 | bytes 12288 | tf_op jit(solution)/shard_map/psum | solution.py:21
  567.6 1.3 fusion.6
  568.9 1.4 exponential_reduce_fusion.4
  570.3 1.3 fusion.7
  571.6 140.1 %pmax.22 = f32[1536]{0:T(1024)S(1)} all-reduce(f32[1536]{0:T(1024)S(1)} %fusion.7), channel_id=1, replica_groups=mesh['rows'=64,'dims'=8] {'rows'}, use_global_device_ids=true, to_apply=%region_10.0 | all-reduce | flops 1536 | bytes 12288 | tf_op jit(solution)/shard_map/pmax | solution.py:20
  711.7 1.4 exponential_reduce_fusion.3
  713.1 141.9 %psum.30 = f32[1536]{0:T(1024)S(1)} all-reduce(f32[1536]{0:T(1024)S(1)} %exponential_reduce_fusion.3), channel_id=1, replica_groups=mesh['rows'=64,'dims'=8] {'rows'}, use_global_device_ids=true, to_apply=%region_12.0 | all-reduce | flops 1536 | bytes 12288 | tf_op jit(solution)/shard_map/psum | solution.py:21
  855.0 1.3 fusion.8
  856.3 1.4 exponential_reduce_fusion.2
  857.7 1.3 fusion.9
  859.0 140.1 %pmax.23 = f32[1536]{0:T(1024)S(1)} all-reduce(f32[1536]{0:T(1024)S(1)} %fusion.9), channel_id=1, replica_groups=mesh['rows'=64,'dims'=8] {'rows'}, use_global_device_ids=true, to_apply=%region_16.0 | all-reduce | flops 1536 | bytes 12288 | tf_op jit(solution)/shard_map/pmax | solution.py:20
  999.2 1.4 exponential_reduce_fusion.1
  1000.5 141.9 %psum.31 = f32[1536]{0:T(1024)S(1)} all-reduce(f32[1536]{0:T(1024)S(1)} %exponential_reduce_fusion.1), channel_id=1, replica_groups=mesh['rows'=64,'dims'=8] {'rows'}, use_global_device_ids=true, to_apply=%region_18.0 | all-reduce | flops 1536 | bytes 12288 | tf_op jit(solution)/shard_map/psum | solution.py:21
  1142.5 0.0 copy-start.1
  1142.5 1.3 fusion.10
  1143.8 1.4 exponential_reduce_fusion
  1145.2 7.8 convolution_convert_fusion
  1152.9 0.0 copy-done.1
  (7 shorter events, 0.1 us)
Async XLA Ops:
  7.2 185.1 %copy-start = (bf16[128,4096]{1,0:T(8,128)(2,1)S(1)}, bf16[128,4096]{1,0:T(8,128)(2,1)}, u32[]{:S(2)}) copy-start(bf16[128,4096]{1,0:T(8,128)(2,1)} %param.2) | copy-start | bytes 3145732
  7.2 178.0 %all-gather.2.cloned.1.call-start = ((), (), s32[]{:S(2)}) async-start(), calls=%async_computation | async-start | bytes 12779520 | tf_op jit(solution)/shard_map/all_gather | solution.py:27
  7.9 267.5 %all-reduce.2.cloned.1.call-start = ((), (), s32[]{:S(2)}) async-start(), calls=%async_computation.1 | async-start | bytes 1572864 | tf_op jit(solution)/shard_map/psum | solution.py:38
  1142.5 10.5 copy-start.1
Sparse Core Ops, SparseCore 0:
  11.0 174.1 all-gather.1
  202.1 73.2 all-reduce.1
where the time goes:
time: 1160 us
  blocking collectives  851 us (73%)
  waiting for transfers between devices  250 us (22%)
  other arithmetic  27.5 us (2%)
  matrix products  17.4 us (1%)
  between operations  14.2 us (1%)
    psum x3, blocking collectives, column_logsumexp(): lax.psum(jnp.sum(jnp.exp(scores - highest[None, :]), axis=0), 'rows')  428 us
    pmax x3, blocking collectives, column_logsumexp(): highest = lax.pmax(highest, 'rows')  422 us
    all_gather x1, waiting for transfers between devices, on_device(): gathered = lax.all_gather(data_latents, 'rows', axis=0, tiled=True)  176 us
    psum x1, waiting for transfers between devices, on_device(): transport = lax.psum(partial_value, 'dims')  73.5 us
  transfers between devices with their start and end apart: 2, of which 2 were waited for; matrix products, arithmetic and copies ran while one was open for 0% of the time, Pallas kernels for 0%

commit v1 on v0

v1 whole, which is shorter than its diff:
```python
import functools
import math

import jax
import jax.numpy as jnp
from jax import lax
from jax.experimental import pallas as pl
from jax.experimental.pallas import tpu as pltpu
from jax.sharding import PartitionSpec as P

ITERS = 3
NZ, NX, NY, NC = 16, 4, 4, 2
PIECES = 6
LAG = 4
NEG = -1e30
MESH = pl.DeviceIdType.MESH
F32, BF16 = jnp.float32, jnp.bfloat16


def logsumexp0(v):
    top = jnp.max(v, axis=0, keepdims=True)
    return top + jnp.log(jnp.sum(jnp.exp(v - top), axis=0, keepdims=True))


def spread(v, n):
    return jnp.transpose(jnp.broadcast_to(v, (n, n)))


def kernel(
    dims_total, x_ref, y_ref, t_ref, pot_ref,
    ysend, yr, xg, yg, x2, part, cx, sm, rs, a1, a2, pb, rbuf, zbuf, xbuf, pbuf, wt, tst,
    y_s, y_r, x_s, x_r, own_sem, ring_s, ring_r, core_s, core_r, sum_s, sum_r,
    row_s, row_r, cz_s, cz_r, cx_s, cx_r, pot_s, pot_r, w_s, w_r, wf_s, wf_r, t_s, t_r, to_sem,
):
    rows_dev, width = x_ref.shape
    quarter = width // NX
    half = quarter // 2
    block_rows = NX * 24
    own_rows = block_rows // NC
    main_rows = NX * 16
    nq = NZ // NY
    mine = nq * own_rows
    padded = a1.shape[0]
    piece = block_rows // PIECES
    columns = NZ * block_rows
    noise = NZ * NX * rows_dev
    entropic = 0.4 / math.sqrt(dims_total)

    r_id, d_id = lax.axis_index("rows"), lax.axis_index("dims")
    z, x = r_id // NX, lax.rem(r_id, NX)
    y, c = d_id // NC, lax.rem(d_id, NC)
    other = NC - 1 - c
    me_xy = x * NY + y

    def at(x_, y_, z_, c_):
        return (z_ * NX + x_, y_ * NC + c_)

    def copy(src, dst, send, recv, to):
        return pltpu.make_async_remote_copy(
            src_ref=src, dst_ref=dst, send_sem=send, recv_sem=recv, device_id=to, device_id_type=MESH
        )

    here = at(x, y, z, c)

    def xy_peer(o):
        return lax.rem(x + o // NY, NX), lax.rem(y + lax.rem(o, NY), NY)

    barrier = pltpu.get_barrier_semaphore()

    def greet(to):
        pl.semaphore_signal(barrier, inc=1, device_id=to, device_id_type=MESH)

    def greet_xy(o, _):
        xt, yt = xy_peer(o)
        greet(at(xt, yt, z, c))
        return 0

    def greet_z(o, _):
        greet(at(x, y, lax.rem(z + o, NZ), c))
        return 0

    def greet_other(o, _):
        greet(at(x, lax.rem(y + o, NY), z, other))
        return 0

    lax.fori_loop(1, NX * NY, greet_xy, 0)
    lax.fori_loop(1, NZ, greet_z, 0)
    lax.fori_loop(0, NY, greet_other, 0)

    wide = y_ref[...].astype(F32)
    for q in range(NX):
        lo = wide[16:24, q * quarter : q * quarter + half]
        hi = wide[16:24, q * quarter + half : (q + 1) * quarter]
        ysend[q, :, 0:quarter] = wide[0:16, q * quarter : (q + 1) * quarter].astype(BF16)
        ysend[q, :, quarter:] = jnp.concatenate([lo, hi], axis=0).astype(BF16)

    pl.semaphore_wait(barrier, (NX * NY - 1) + (NZ - 1) + NY)

    def y_copy(o):
        xt = lax.rem(x + o, NX)
        return copy(ysend.at[xt], yr.at[x], y_s.at[o - 1], y_r.at[o - 1], at(xt, y, z, c))

    def x_copy(o):
        xt = lax.rem(x + o, NX)
        cols = pl.ds(pl.multiple_of(xt * quarter, quarter), quarter)
        return copy(x_ref.at[:, cols], xg.at[x], x_s.at[o - 1], x_r.at[o - 1], at(xt, y, z, c))

    for o in range(1, NX):
        y_copy(o).start()
    for o in range(1, NX):
        x_copy(o).start()
    own_x = pltpu.make_async_copy(
        x_ref.at[:, pl.ds(pl.multiple_of(x * quarter, quarter), quarter)], xg.at[x], own_sem.at[0]
    )
    own_x.start()
    yr[x] = ysend[x]
    for o in range(1, NX):
        y_copy(o).wait()

    def slot(z_):
        return lax.rem(z_, NY) * nq + z_ // NY

    mid = slot(z)
    tails = []
    for s in range(NX):
        yg[mid, s * 16 : (s + 1) * 16, :] = yr[s, :, 0:quarter]
        tail = yr[s, :, quarter:].astype(F32)
        tails.append(jnp.concatenate([tail[0:8], tail[8:16]], axis=1))
    yg[mid, main_rows:block_rows, :] = jnp.concatenate(tails, axis=0).astype(BF16)

    def ring_copy(way, step, u, z_):
        rows = pl.ds(pl.multiple_of(u * piece, piece), piece)
        ref = yg.at[slot(z_), rows]
        to = lax.rem(z + 1, NZ) if way == 0 else lax.rem(z + NZ - 1, NZ)
        return copy(ref, ref, ring_s.at[way, step - 1, u], ring_r.at[way, step - 1, u], at(x, y, to, c))

    def origin(way, step):
        return lax.rem(z + NZ - step, NZ) if way == 0 else lax.rem(z + step, NZ)

    last = NZ // 2

    def ring_first(u, _):
        for way in range(2):
            ring_copy(way, 1, u, z).start()
        return 0

    lax.fori_loop(0, PIECES, ring_first, 0)

    def pass_on(step, u):
        for way in range(2):
            ring_copy(way, step, u, origin(way, step)).wait_recv()

            @pl.when((step < last - 1) | ((u < PIECES // 2) == (way == 0)))
            def _():
                ring_copy(way, step + 1, u, origin(way, step)).start()

    def source(b):
        away = (b + 1) // 2
        return lax.rem(jnp.where(lax.rem(b, 2) == 1, z + away, z + NZ - away), NZ)

    def core_copy(s):
        return copy(part.at[s, other], cx.at[s], core_s.at[s], core_r.at[s], at(x, y, z, other))

    def distance(b):
        s = slot(source(b))
        rows = yg[s]
        noise_block = xg[...].reshape(NX * rows_dev, quarter)
        products = lax.dot_general(rows, noise_block, (((1,), (1,)), ((), ())), preferred_element_type=F32)
        tall = rows.astype(F32)
        data_sq = jnp.sum(tall * tall, axis=1, keepdims=True)
        value = (x2[0:1, :] + data_sq - 2.0 * products) * (1.0 / dims_total)
        for k in range(NC):
            part[s, k] = value[k * own_rows : (k + 1) * own_rows]
        core_copy(s).start()

    def sum_copy(s, o, zs):
        xt = lax.rem(x + o, NX)
        return copy(
            sm.at[s, xt], rs.at[me_xy, zs // NY], sum_s.at[s, o], sum_r.at[me_xy, zs // NY],
            at(xt, lax.rem(zs, NY), z, c),
        )

    def hand_out(b):
        zs = source(b)
        s = slot(zs)
        core_copy(s).wait()
        value = part[s, c] + cx[s]
        for k in range(NX):
            sm[s, k] = value[:, k * rows_dev : (k + 1) * rows_dev]
        for o in range(1, NX):
            sum_copy(s, o, zs).start()

        @pl.when(lax.rem(zs, NY) == y)
        def _():
            rs[me_xy, zs // NY] = sm[s, x]

        @pl.when(lax.rem(zs, NY) != y)
        def _():
            sum_copy(s, 0, zs).start()

    def early(step, _):
        def each(u, _):
            pass_on(step, u)
            return 0

        return lax.fori_loop(0, PIECES, each, 0)

    lax.fori_loop(1, LAG, early, 0)

    own_x.wait()
    for o in range(1, NX):
        x_copy(o).wait()
    for s in range(NX):
        tall = xg[s].astype(F32)
        norm = jnp.sum(tall * tall, axis=1, keepdims=True)
        flat = jnp.transpose(jnp.broadcast_to(norm, (rows_dev, rows_dev)))
        x2[:, s * rows_dev : (s + 1) * rows_dev] = flat[0:8]

    blocks = NZ - 1
    per = PIECES // 2

    def work(step, i):
        b = (step - LAG) * per + i

        @pl.when(b < blocks)
        def _():
            distance(b)

        @pl.when((b >= per) & (b - per < blocks))
        def _():
            hand_out(b - per)

    def later(step, _):
        def each(i, _):
            pass_on(step, 2 * i)
            pass_on(step, 2 * i + 1)
            work(step, i)
            return 0

        return lax.fori_loop(0, per, each, 0)

    lax.fori_loop(LAG, last, later, 0)
    far = lax.rem(z + last, NZ)

    def ring_last(i, _):
        ring_copy(0, last, i, far).wait_recv()
        ring_copy(1, last, i + per, far).wait_recv()
        work(last, i)
        return 0

    lax.fori_loop(0, per, ring_last, 0)
    done = (last + 1 - LAG) * per

    def rest(b, _):
        hand_out(b)
        return 0

    def rest_distance(b, _):
        distance(b)
        return 0

    lax.fori_loop(min(done, blocks), blocks, rest_distance, 0)
    lax.fori_loop(min(done - per, blocks), blocks, rest, 0)
    distance(NZ - 1)

    def ring_sent(step, _):
        def each(u, _):
            for way in range(2):
                @pl.when((step < last) | ((u < PIECES // 2) == (way == 0)))
                def _():
                    ring_copy(way, step, u, z).wait_send()
            return 0

        return lax.fori_loop(0, PIECES, each, 0)

    lax.fori_loop(1, last + 1, ring_sent, 0)
    hand_out(NZ - 1)

    def sums_sent(zs, _):
        for o in range(1, NX):
            sum_copy(slot(zs), o, zs).wait_send()

        @pl.when(lax.rem(zs, NY) != y)
        def _():
            sum_copy(slot(zs), 0, zs).wait_send()

        return 0

    lax.fori_loop(0, NZ, sums_sent, 0)

    def sums_in(src, _):
        @pl.when(src != me_xy)
        def _():
            for q in range(nq):
                copy(rs.at[src, q], rs.at[src, q], sum_s.at[0, 0], sum_r.at[src, q], here).wait_recv()

        return 0

    lax.fori_loop(0, NX * NY, sums_in, 0)
    for q in range(nq):
        total = rs[0, q]
        for src in range(1, NX * NY):
            total = total + rs[src, q]
        a1[q * own_rows : (q + 1) * own_rows, :] = total * (-1.0 / entropic)
    if padded > mine:
        a1[mine:padded, :] = jnp.full((padded - mine, rows_dev), NEG, F32)
    for h in range(padded // rows_dev):
        cut = slice(h * rows_dev, (h + 1) * rows_dev)
        a2[:, cut] = jnp.transpose(a1[cut, :])
    pb[...] = jnp.zeros_like(pb)

    def exchange(buf, it, me, n, peer, send, recv):
        def desc(i, who):
            return copy(buf.at[it, who], buf.at[it, who], send.at[it, i - 1], recv.at[it, i - 1], peer(lax.rem(me + i, n)))

        def begin(i, _):
            desc(i, me).start()
            return 0

        def sent(i, _):
            desc(i, me).wait_send()
            return 0

        def end(i, _):
            desc(i, lax.rem(me + n - i, n)).wait_recv()
            return 0

        lax.fori_loop(1, n, begin, 0)
        lax.fori_loop(1, n, sent, 0)
        lax.fori_loop(1, n, end, 0)
        return logsumexp0(buf[it])[0]

    def yc_peer(k):
        return at(x, k // NC, z, lax.rem(k, NC))

    def row_total(it):
        rbuf[it, d_id] = logsumexp0(a1[...] + pb[...])
        return exchange(rbuf, it, d_id, NY * NC, yc_peer, row_s, row_r)

    real = lax.broadcasted_iota(jnp.int32, (1, padded), 1) < mine

    def iteration(it, _):
        row = spread(math.log(columns) - row_total(it), rows_dev)
        for h in range(padded // rows_dev):
            cut = slice(h * rows_dev, (h + 1) * rows_dev)
            zbuf[it, z, :, cut] = logsumexp0(a2[:, cut] + row)
        xbuf[it, x] = exchange(zbuf, it, z, NZ, lambda k: at(x, y, k, c), cz_s, cz_r)
        total = exchange(xbuf, it, x, NX, lambda k: at(k, y, z, c), cx_s, cx_r)
        p = jnp.where(real, math.log(noise) - total, 0.0)
        pbuf[0, d_id] = p
        for h in range(padded // rows_dev):
            cut = slice(h * rows_dev, (h + 1) * rows_dev)
            pb[cut, :] = spread(p[:, cut], rows_dev)
        return 0

    lax.fori_loop(0, ITERS, iteration, 0)

    def pot_copy(i, who):
        return copy(
            pbuf.at[0, who], pbuf.at[0, who], pot_s.at[i - 1], pot_r.at[i - 1], yc_peer(lax.rem(d_id + i, NY * NC))
        )

    def pot_begin(i, _):
        pot_copy(i, d_id).start()
        return 0

    norm = row_total(ITERS)
    lax.fori_loop(1, NY * NC, pot_begin, 0)
    weights = jnp.exp(a1[0:mine, :] + pb[0:mine, :] - norm)
    wt[x, y, :, c] = weights.reshape(nq, own_rows, rows_dev).astype(BF16)

    def w_copy(o, xs, ys):
        xt, yt = xy_peer(o)
        ref = wt.at[xs, ys, :, c]
        return copy(ref, ref, w_s.at[o - 1], w_r.at[o - 1], at(xt, yt, z, c))

    def w_begin(o, _):
        w_copy(o, x, y).start()
        return 0

    lax.fori_loop(1, NX * NY, w_begin, 0)

    def wf_copy(o, core):
        ref = wt.at[lax.rem(x + o, NX), :, :, core]
        return copy(ref, ref, wf_s.at[o], wf_r.at[o], at(x, y, z, other))

    def relay(i, _):
        o = NX - 1 - i
        xs = lax.rem(x + o, NX)
        back = lax.rem(NX - o, NX)

        def arrive(dy, _):
            k = back * NY + dy

            @pl.when(k > 0)
            def _():
                w_copy(k, xs, lax.rem(y + NY - dy, NY)).wait_recv()

            return 0

        lax.fori_loop(0, NY, arrive, 0)
        wf_copy(o, c).start()
        return 0

    def t_copy(o):
        xt = lax.rem(x + o, NX)
        cols = pl.ds(pl.multiple_of(x * quarter, quarter), quarter)
        return copy(tst.at[o], t_ref.at[:, cols], t_s.at[o], t_r.at[o], at(xt, y, z, c))

    own_t = pltpu.make_async_copy(
        tst.at[0], t_ref.at[:, pl.ds(pl.multiple_of(x * quarter, quarter), quarter)], to_sem.at[0]
    )

    def target(i, _):
        o = NX - 1 - i
        xs = lax.rem(x + o, NX)
        wf_copy(o, other).wait_recv()
        w = wt[xs].reshape(columns, rows_dev)
        value = lax.dot_general(
            w, yg[...].reshape(columns, quarter), (((0,), (0,)), ((), ())), preferred_element_type=F32
        )
        tst[o] = value.astype(BF16)

        @pl.when(o > 0)
        def _():
            t_copy(o).start()

        @pl.when(o == 0)
        def _():
            own_t.start()

        return 0

    lax.fori_loop(0, NX, relay, 0)
    lax.fori_loop(0, NX, target, 0)

    def w_sent(o, _):
        w_copy(o, x, y).wait_send()
        return 0

    lax.fori_loop(1, NX * NY, w_sent, 0)

    def wf_sent(o, _):
        wf_copy(o, c).wait_send()
        return 0

    lax.fori_loop(0, NX, wf_sent, 0)

    def pot_end(i, _):
        pot_copy(i, d_id).wait_send()
        pot_copy(i, lax.rem(d_id + NY * NC - i, NY * NC)).wait_recv()
        return 0

    lax.fori_loop(1, NY * NC, pot_end, 0)
    pot_ref[...] = pbuf[0] * entropic
    own_t.wait()
    for o in range(1, NX):
        t_copy(o).wait()


def on_device(noise_latents, data_latents):
    rows_dev, width = noise_latents.shape
    quarter = width // NX
    block_rows = NX * 24
    own_rows = block_rows // NC
    nq = NZ // NY
    mine = nq * own_rows
    padded = -(-mine // rows_dev) * rows_dev
    nd = NY * NC
    dma = pltpu.SemaphoreType.DMA
    last = NZ // 2
    sems = [
        (NX - 1,), (NX - 1,), (NX - 1,), (NX - 1,), (1,),
        (2, last, PIECES), (2, last, PIECES), (NZ,), (NZ,), (NZ, NX), (NX * NY, nq),
        (ITERS + 1, nd - 1), (ITERS + 1, nd - 1), (ITERS, NZ - 1), (ITERS, NZ - 1), (ITERS, NX - 1), (ITERS, NX - 1),
        (nd - 1,), (nd - 1,), (NX * NY - 1,), (NX * NY - 1,), (NX,), (NX,), (NX,), (NX,), (1,),
    ]
    targets, pots = pl.pallas_call(
        functools.partial(kernel, width * nd),
        out_shape=(
            jax.ShapeDtypeStruct((rows_dev, width), BF16),
            jax.ShapeDtypeStruct((nd, 1, padded), F32),
        ),
        in_specs=[pl.BlockSpec(memory_space=pl.ANY), pl.BlockSpec(memory_space=pltpu.VMEM)],
        out_specs=(pl.BlockSpec(memory_space=pl.ANY), pl.BlockSpec(memory_space=pltpu.VMEM)),
        scratch_shapes=[
            pltpu.VMEM((NX, 16, quarter * 3 // 2), BF16),
            pltpu.VMEM((NX, 16, quarter * 3 // 2), BF16),
            pltpu.VMEM((NX, rows_dev, quarter), BF16),
            pltpu.VMEM((NZ, block_rows, quarter), BF16),
            pltpu.VMEM((8, NX * rows_dev), F32),
            pltpu.VMEM((NZ, NC, own_rows, NX * rows_dev), F32),
            pltpu.VMEM((NZ, own_rows, NX * rows_dev), F32),
            pltpu.VMEM((NZ, NX, own_rows, rows_dev), F32),
            pltpu.VMEM((NX * NY, nq, own_rows, rows_dev), F32),
            pltpu.VMEM((padded, rows_dev), F32),
            pltpu.VMEM((rows_dev, padded), F32),
            pltpu.VMEM((padded, rows_dev), F32),
            pltpu.VMEM((ITERS + 1, nd, 1, rows_dev), F32),
            pltpu.VMEM((ITERS, NZ, 1, padded), F32),
            pltpu.VMEM((ITERS, NX, 1, padded), F32),
            pltpu.VMEM((1, nd, 1, padded), F32),
            pltpu.VMEM((NX, NY, nq, NC, own_rows, rows_dev), BF16),
            pltpu.VMEM((NX, rows_dev, quarter), BF16),
        ]
        + [dma(shape) for shape in sems],
        compiler_params=pltpu.CompilerParams(
            collective_id=0, has_side_effects=True, vmem_limit_bytes=48 * 1024 * 1024
        ),
    )(noise_latents, data_latents)
    flat = pots[:, 0, :mine].reshape(NY, NC, nq, own_rows).transpose(2, 0, 1, 3).reshape(NZ, block_rows)
    main = flat[:, : NX * 16].reshape(NZ, NX, 16)
    tail = flat[:, NX * 16 :].reshape(NZ, NX, 8)
    return targets, jnp.concatenate([main, tail], axis=2).reshape(-1)


def solution(mesh):
    placed = (P("rows", "dims"), P("rows", "dims"))
    return jax.shard_map(
        on_device, mesh=mesh, in_specs=placed, out_specs=(P("rows", "dims"), P()), check_vma=False
    )
```

time: 1160 us -> 152 us (0.13)
  the two profiles are of different devices: /device:TPU:2 before, /device:TPU:1 now
where the time goes in v1:
time: 152 us
  Pallas kernels  147 us (97%)
  local copies, waits for them, and re-layouts  4.32 us (3%)
    pallas_call x1, Pallas kernels, on_device(): pl.pallas_call(functools.partial(kernel, width * nd), out_shape=(jax.Shap...  147 us
    unnamed x5, local copies, waits for them, and re-layouts  3.11 us

profile of v1, /device:TPU:1, one launch (start us, length us, event | category | flops | bytes accessed | tf_op | source)
XLA Modules:
  0.0 152.2 jit_solution(17370988570757296704)
XLA Ops:
  0.6 0.0 copy-start
  0.6 1.2 copy-done
  1.9 0.0 copy-start.1
  1.9 0.9 copy-done.1
  2.8 147.2 %shard_map.41 = (bf16[128,4096]{1,0:T(8,128)(2,1)S(1)}, f32[8,1,256]{2,1,0:T(1,128)S(1)}) custom-call(bf16[128,4096]{1,0:T(8,128)(2,1)S(1)} %copy-done, bf16[24,4096]{1,0:T(8,128)(2,1)S(1)} %copy-done.1), custom_call_target="tpu_custom_call" | custom-call | tf_op jit(solution)/shard_map/pallas_call | solution.py:478
  150.0 0.1 reshape_squeeze.3
  150.1 0.1 reshape.16
  150.2 0.1 slice.13
  150.2 0.1 copy.5
  150.3 0.1 copy.6
  150.4 0.1 reshape.17
  150.5 0.1 pad_maximum_fusion
  150.6 0.7 reshape.19
  151.3 1.0 copy.10
  (2 shorter events, 0.0 us)
Async XLA Ops:
  0.6 1.2 copy-start
  1.9 0.9 copy-start.1

commit v2 on v1

--- a/solution.py
+++ b/solution.py
@@ -11,7 +11,7 @@
 ITERS = 3
 NZ, NX, NY, NC = 16, 4, 4, 2
 PIECES = 6
-LAG = 4
+LAG = 3
 NEG = -1e30
 MESH = pl.DeviceIdType.MESH
 F32, BF16 = jnp.float32, jnp.bfloat16
@@ -28,16 +28,15 @@
 
 def kernel(
     dims_total, x_ref, y_ref, t_ref, pot_ref,
-    ysend, yr, xg, yg, x2, part, cx, sm, rs, a1, a2, pb, rbuf, zbuf, xbuf, pbuf, wt, tst,
+    ybuf, ysend, yr, xg, yg, x2, part, cx, sm, rs, a1, a2, pb, rbuf, zbuf, xbuf, pbuf, full, pall, wt, tst,
     y_s, y_r, x_s, x_r, own_sem, ring_s, ring_r, core_s, core_r, sum_s, sum_r,
-    row_s, row_r, cz_s, cz_r, cx_s, cx_r, pot_s, pot_r, w_s, w_r, wf_s, wf_r, t_s, t_r, to_sem,
+    row_s, row_r, cz_s, cz_r, cx_s, cx_r, pot_s, pot_r, one_s, one_r, set_s, set_r, core2_s, core2_r, t_s, t_r, to_sem,
 ):
     rows_dev, width = x_ref.shape
     quarter = width // NX
     half = quarter // 2
     block_rows = NX * 24
     own_rows = block_rows // NC
-    main_rows = NX * 16
     nq = NZ // NY
     mine = nq * own_rows
     padded = a1.shape[0]
@@ -65,36 +64,31 @@
     def xy_peer(o):
         return lax.rem(x + o // NY, NX), lax.rem(y + lax.rem(o, NY), NY)
 
+    fetch = pltpu.make_async_copy(y_ref, ybuf, own_sem.at[1])
+    fetch.start()
+
     barrier = pltpu.get_barrier_semaphore()
 
     def greet(to):
         pl.semaphore_signal(barrier, inc=1, device_id=to, device_id_type=MESH)
 
-    def greet_xy(o, _):
-        xt, yt = xy_peer(o)
-        greet(at(xt, yt, z, c))
-        return 0
-
-    def greet_z(o, _):
-        greet(at(x, y, lax.rem(z + o, NZ), c))
-        return 0
-
-    def greet_other(o, _):
-        greet(at(x, lax.rem(y + o, NY), z, other))
-        return 0
-
-    lax.fori_loop(1, NX * NY, greet_xy, 0)
-    lax.fori_loop(1, NZ, greet_z, 0)
-    lax.fori_loop(0, NY, greet_other, 0)
-
-    wide = y_ref[...].astype(F32)
+    for o in range(1, NX):
+        greet(at(lax.rem(x + o, NX), y, z, c))
+    for o in range(1, NY):
+        greet(at(x, lax.rem(y + o, NY), z, c))
+    greet(at(x, y, lax.rem(z + 1, NZ), c))
+    greet(at(x, y, lax.rem(z + NZ - 1, NZ), c))
+    greet(at(x, y, z, other))
+
+    fetch.wait()
+    wide = ybuf[...].astype(F32)
     for q in range(NX):
         lo = wide[16:24, q * quarter : q * quarter + half]
         hi = wide[16:24, q * quarter + half : (q + 1) * quarter]
         ysend[q, :, 0:quarter] = wide[0:16, q * quarter : (q + 1) * quarter].astype(BF16)
         ysend[q, :, quarter:] = jnp.concatenate([lo, hi], axis=0).astype(BF16)
 
-    pl.semaphore_wait(barrier, (NX * NY - 1) + (NZ - 1) + NY)
+    pl.semaphore_wait(barrier, (NX - 1) + (NY - 1) + 2 + 1)
 
     def y_copy(o):
         xt = lax.rem(x + o, NX)
@@ -121,12 +115,12 @@
         return lax.rem(z_, NY) * nq + z_ // NY
 
     mid = slot(z)
-    tails = []
-    for s in range(NX):
-        yg[mid, s * 16 : (s + 1) * 16, :] = yr[s, :, 0:quarter]
-        tail = yr[s, :, quarter:].astype(F32)
-        tails.append(jnp.concatenate([tail[0:8], tail[8:16]], axis=1))
-    yg[mid, main_rows:block_rows, :] = jnp.concatenate(tails, axis=0).astype(BF16)
+    pieces = []
+    for k in range(NX):
+        rows = yr[k].astype(F32)
+        pieces.append(rows[:, 0:quarter])
+        pieces.append(jnp.concatenate([rows[0:8, quarter:], rows[8:16, quarter:]], axis=1))
+    yg[mid] = jnp.concatenate(pieces, axis=0).astype(BF16)
 
     def ring_copy(way, step, u, z_):
         rows = pl.ds(pl.multiple_of(u * piece, piece), piece)
@@ -220,9 +214,9 @@
     per = PIECES // 2
 
     def work(step, i):
-        b = (step - LAG) * per + i
-
-        @pl.when(b < blocks)
+        b = (step - LAG) * per + i - 1
+
+        @pl.when((b >= 0) & (b < blocks))
         def _():
             distance(b)
 
@@ -249,7 +243,7 @@
         return 0
 
     lax.fori_loop(0, per, ring_last, 0)
-    done = (last + 1 - LAG) * per
+    done = (last + 1 - LAG) * per - 1
 
     def rest(b, _):
         hand_out(b)
@@ -260,7 +254,7 @@
         return 0
 
     lax.fori_loop(min(done, blocks), blocks, rest_distance, 0)
-    lax.fori_loop(min(done - per, blocks), blocks, rest, 0)
+    lax.fori_loop(max(min(done - per, blocks), 0), blocks, rest, 0)
     distance(NZ - 1)
 
     def ring_sent(step, _):
@@ -309,7 +303,7 @@
         a2[:, cut] = jnp.transpose(a1[cut, :])
     pb[...] = jnp.zeros_like(pb)
 
-    def exchange(buf, it, me, n, peer, send, recv):
+    def exchange(buf, it, me, n, peer, send, recv, beside=lambda: None):
         def desc(i, who):
             return copy(buf.at[it, who], buf.at[it, who], send.at[it, i - 1], recv.at[it, i - 1], peer(lax.rem(me + i, n)))
 
@@ -326,81 +320,134 @@
             return 0
 
         lax.fori_loop(1, n, begin, 0)
+        beside()
         lax.fori_loop(1, n, sent, 0)
         lax.fori_loop(1, n, end, 0)
-        return logsumexp0(buf[it])[0]
+        return buf[it]
 
     def yc_peer(k):
         return at(x, k // NC, z, lax.rem(k, NC))
 
     def row_total(it):
         rbuf[it, d_id] = logsumexp0(a1[...] + pb[...])
-        return exchange(rbuf, it, d_id, NY * NC, yc_peer, row_s, row_r)
+        return logsumexp0(exchange(rbuf, it, d_id, NY * NC, yc_peer, row_s, row_r))[0]
+
+    full[c, x, y] = a1[0:mine, :]
+    plane = ((NY, y, NX, x), (NX, x, NY, y))
+
+    def peer_of(core, along_first, o):
+        if (core == 0) == along_first:
+            return at(x, lax.rem(y + o, NY), z, c)
+        return at(lax.rem(x + o, NX), y, z, c)
+
+    def one_copy(core, o, back):
+        n, pos = plane[core][0:2]
+        src = lax.rem(pos + n - o, n) if back else pos
+        ref = full.at[0, x, src] if core == 0 else full.at[1, src, y]
+        return copy(ref, ref, one_s.at[o - 1], one_r.at[o - 1], peer_of(core, True, o))
+
+    def set_ref(core, o):
+        n, pos = plane[core][2:4]
+        src = lax.rem(pos + n - o, n)
+        return full.at[0, src] if core == 0 else full.at[1, :, src]
+
+    def set_copy(core, o, back):
+        ref = set_ref(core, o if back else 0)
+        return copy(ref, ref, set_s.at[o - 1], set_r.at[o - 1], peer_of(core, False, o))
+
+    def over_copy(core, o):
+        ref = set_ref(core, o)
+        return copy(ref, ref, core2_s.at[o], core2_r.at[o], at(x, y, z, other))
+
+    def by_core(step):
+        for core in range(NC):
+            @pl.when(c == core)
+            def _():
+                step(core)
+
+    def near(n):
+        return sorted({1, n - 1})
+
+    def distant(n):
+        return range(2, n - 1)
+
+    def first_part(core):
+        for o in range(1, plane[core][0]):
+            one_copy(core, o, False).start()
+
+    def second_part(core):
+        for o in range(1, plane[core][0]):
+            one_copy(core, o, True).wait_recv()
+        for o in near(plane[core][2]):
+            set_copy(core, o, False).start()
+        over_copy(core, 0).start()
+
+    def third_part(core):
+        for o in distant(plane[core][2]):
+            set_copy(core, o, False).start()
+        for o in near(plane[core][2]):
+            set_copy(core, o, True).wait_recv()
+            over_copy(core, o).start()
+
+    def last_part(core):
+        for o in distant(plane[core][2]):
+            set_copy(core, o, True).wait_recv()
+            over_copy(core, o).start()
+
+    def all_in(core):
+        for o in range(plane[1 - core][2]):
+            over_copy(1 - core, o).wait_recv()
+
+    def all_out(core):
+        for o in range(1, plane[core][0]):
+            one_copy(core, o, False).wait_send()
+        for o in range(1, plane[core][2]):
+            set_copy(core, o, False).wait_send()
+        for o in range(plane[core][2]):
+            over_copy(core, o).wait_send()
+
+    def spread_scores(it):
+        for k, part_of in enumerate((first_part, second_part, third_part)):
+            @pl.when(it == k)
+            def _():
+                by_core(part_of)
 
     real = lax.broadcasted_iota(jnp.int32, (1, padded), 1) < mine
 
-    def iteration(it, _):
+    def columns_along_z(it):
         row = spread(math.log(columns) - row_total(it), rows_dev)
         for h in range(padded // rows_dev):
             cut = slice(h * rows_dev, (h + 1) * rows_dev)
             zbuf[it, z, :, cut] = logsumexp0(a2[:, cut] + row)
-        xbuf[it, x] = exchange(zbuf, it, z, NZ, lambda k: at(x, y, k, c), cz_s, cz_r)
-        total = exchange(xbuf, it, x, NX, lambda k: at(k, y, z, c), cx_s, cx_r)
+        return logsumexp0(
+            exchange(zbuf, it, z, NZ, lambda k: at(x, y, k, c), cz_s, cz_r, lambda: spread_scores(it))
+        )[0]
+
+    def iteration(it, _):
+        xbuf[it, x] = columns_along_z(it)
+        total = logsumexp0(exchange(xbuf, it, x, NX, lambda k: at(k, y, z, c), cx_s, cx_r))[0]
         p = jnp.where(real, math.log(noise) - total, 0.0)
-        pbuf[0, d_id] = p
         for h in range(padded // rows_dev):
             cut = slice(h * rows_dev, (h + 1) * rows_dev)
             pb[cut, :] = spread(p[:, cut], rows_dev)
         return 0
 
-    lax.fori_loop(0, ITERS, iteration, 0)
-
-    def pot_copy(i, who):
-        return copy(
-            pbuf.at[0, who], pbuf.at[0, who], pot_s.at[i - 1], pot_r.at[i - 1], yc_peer(lax.rem(d_id + i, NY * NC))
-        )
-
-    def pot_begin(i, _):
-        pot_copy(i, d_id).start()
-        return 0
-
-    norm = row_total(ITERS)
-    lax.fori_loop(1, NY * NC, pot_begin, 0)
-    weights = jnp.exp(a1[0:mine, :] + pb[0:mine, :] - norm)
-    wt[x, y, :, c] = weights.reshape(nq, own_rows, rows_dev).astype(BF16)
-
-    def w_copy(o, xs, ys):
-        xt, yt = xy_peer(o)
-        ref = wt.at[xs, ys, :, c]
-        return copy(ref, ref, w_s.at[o - 1], w_r.at[o - 1], at(xt, yt, z, c))
-
-    def w_begin(o, _):
-        w_copy(o, x, y).start()
-        return 0
-
-    lax.fori_loop(1, NX * NY, w_begin, 0)
-
-    def wf_copy(o, core):
-        ref = wt.at[lax.rem(x + o, NX), :, :, core]
-        return copy(ref, ref, wf_s.at[o], wf_r.at[o], at(x, y, z, other))
-
-    def relay(i, _):
-        o = NX - 1 - i
-        xs = lax.rem(x + o, NX)
-        back = lax.rem(NX - o, NX)
-
-        def arrive(dy, _):
-            k = back * NY + dy
-
-            @pl.when(k > 0)
-            def _():
-                w_copy(k, xs, lax.rem(y + NY - dy, NY)).wait_recv()
-
-            return 0
-
-        lax.fori_loop(0, NY, arrive, 0)
-        wf_copy(o, c).start()
-        return 0
+    lax.fori_loop(0, ITERS - 1, iteration, 0)
+
+    me_plane = x * NY * NC + d_id
+    pbuf[0, me_plane] = columns_along_z(ITERS - 1)
+    found = exchange(
+        pbuf, 0, me_plane, NX * NY * NC, lambda k: (z * NX + k // (NY * NC), lax.rem(k, NY * NC)),
+        pot_s, pot_r, lambda: by_core(last_part),
+    )
+    pots = math.log(noise) - logsumexp0(found.reshape(NX, NY * NC, 1, padded))[0]
+    pot_ref[...] = pots * entropic
+    for k in range(NY * NC):
+        for h in range(padded // rows_dev):
+            lo, hi = h * rows_dev, min((h + 1) * rows_dev, mine)
+            pall[k % NC * NY + k // NC, lo:hi, :] = spread(pots[k, :, lo : lo + rows_dev], rows_dev)[0 : hi - lo]
+
+    by_core(all_in)
 
     def t_copy(o):
         xt = lax.rem(x + o, NX)
@@ -412,10 +459,15 @@
     )
 
     def target(i, _):
-        o = NX - 1 - i
+        o = lax.rem(NX // 2 + i, NX)
         xs = lax.rem(x + o, NX)
-        wf_copy(o, other).wait_recv()
-        w = wt[xs].reshape(columns, rows_dev)
+        scores = jnp.concatenate([full[k, xs] for k in range(NC)], axis=0) + pall[...]
+        top = jnp.max(jnp.max(scores, axis=0), axis=0, keepdims=True)
+        powers = jnp.exp(scores - top)
+        weights = powers * (1.0 / jnp.sum(jnp.sum(powers, axis=0), axis=0, keepdims=True))
+        for k in range(NY * NC):
+            wt[k % NY, :, k // NY] = weights[k].reshape(nq, own_rows, rows_dev).astype(BF16)
+        w = wt[...].reshape(columns, rows_dev)
         value = lax.dot_general(
             w, yg[...].reshape(columns, quarter), (((0,), (0,)), ((), ())), preferred_element_type=F32
         )
@@ -431,28 +483,9 @@
 
         return 0
 
-    lax.fori_loop(0, NX, relay, 0)
     lax.fori_loop(0, NX, target, 0)
 
-    def w_sent(o, _):
-        w_copy(o, x, y).wait_send()
-        return 0
-
-    lax.fori_loop(1, NX * NY, w_sent, 0)
-
-    def wf_sent(o, _):
-        wf_copy(o, c).wait_send()
-        return 0
-
-    lax.fori_loop(0, NX, wf_sent, 0)
-
-    def pot_end(i, _):
-        pot_copy(i, d_id).wait_send()
-        pot_copy(i, lax.rem(d_id + NY * NC - i, NY * NC)).wait_recv()
-        return 0
-
-    lax.fori_loop(1, NY * NC, pot_end, 0)
-    pot_ref[...] = pbuf[0] * entropic
+    by_core(all_out)
     own_t.wait()
     for o in range(1, NX):
         t_copy(o).wait()
@@ -469,11 +502,13 @@
     nd = NY * NC
     dma = pltpu.SemaphoreType.DMA
     last = NZ // 2
+    longest = max(NX, NY)
     sems = [
-        (NX - 1,), (NX - 1,), (NX - 1,), (NX - 1,), (1,),
+        (NX - 1,), (NX - 1,), (NX - 1,), (NX - 1,), (2,),
         (2, last, PIECES), (2, last, PIECES), (NZ,), (NZ,), (NZ, NX), (NX * NY, nq),
-        (ITERS + 1, nd - 1), (ITERS + 1, nd - 1), (ITERS, NZ - 1), (ITERS, NZ - 1), (ITERS, NX - 1), (ITERS, NX - 1),
-        (nd - 1,), (nd - 1,), (NX * NY - 1,), (NX * NY - 1,), (NX,), (NX,), (NX,), (NX,), (1,),
+        (ITERS, nd - 1), (ITERS, nd - 1), (ITERS, NZ - 1), (ITERS, NZ - 1), (ITERS - 1, NX - 1), (ITERS - 1, NX - 1),
+        (1, NX * nd - 1), (1, NX * nd - 1),
+        (longest,), (longest,), (longest,), (longest,), (longest,), (longest,), (NX,), (NX,), (1,),
     ]
     targets, pots = pl.pallas_call(
         functools.partial(kernel, width * nd),
@@ -481,9 +516,10 @@
             jax.ShapeDtypeStruct((rows_dev, width), BF16),
             jax.ShapeDtypeStruct((nd, 1, padded), F32),
         ),
-        in_specs=[pl.BlockSpec(memory_space=pl.ANY), pl.BlockSpec(memory_space=pltpu.VMEM)],
+        in_specs=[pl.BlockSpec(memory_space=pl.ANY)] * 2,
         out_specs=(pl.BlockSpec(memory_space=pl.ANY), pl.BlockSpec(memory_space=pltpu.VMEM)),
         scratch_shapes=[
+            pltpu.VMEM(data_latents.shape, BF16),
             pltpu.VMEM((NX, 16, quarter * 3 // 2), BF16),
             pltpu.VMEM((NX, 16, quarter * 3 // 2), BF16),
             pltpu.VMEM((NX, rows_dev, quarter), BF16),
@@ -496,22 +532,22 @@
             pltpu.VMEM((padded, rows_dev), F32),
             pltpu.VMEM((rows_dev, padded), F32),
             pltpu.VMEM((padded, rows_dev), F32),
-            pltpu.VMEM((ITERS + 1, nd, 1, rows_dev), F32),
+            pltpu.VMEM((ITERS, nd, 1, rows_dev), F32),
             pltpu.VMEM((ITERS, NZ, 1, padded), F32),
-            pltpu.VMEM((ITERS, NX, 1, padded), F32),
-            pltpu.VMEM((1, nd, 1, padded), F32),
-            pltpu.VMEM((NX, NY, nq, NC, own_rows, rows_dev), BF16),
+            pltpu.VMEM((ITERS - 1, NX, 1, padded), F32),
+            pltpu.VMEM((1, NX * nd, 1, padded), F32),
+            pltpu.VMEM((NC, NX, NY, mine, rows_dev), F32),
+            pltpu.VMEM((nd, mine, rows_dev), F32),
+            pltpu.VMEM((NY, nq, NC, own_rows, rows_dev), BF16),
             pltpu.VMEM((NX, rows_dev, quarter), BF16),
         ]
         + [dma(shape) for shape in sems],
         compiler_params=pltpu.CompilerParams(
-            collective_id=0, has_side_effects=True, vmem_limit_bytes=48 * 1024 * 1024
+            collective_id=0, has_side_effects=True, vmem_limit_bytes=60 * 1024 * 1024
         ),
     )(noise_latents, data_latents)
-    flat = pots[:, 0, :mine].reshape(NY, NC, nq, own_rows).transpose(2, 0, 1, 3).reshape(NZ, block_rows)
-    main = flat[:, : NX * 16].reshape(NZ, NX, 16)
-    tail = flat[:, NX * 16 :].reshape(NZ, NX, 8)
-    return targets, jnp.concatenate([main, tail], axis=2).reshape(-1)
+    flat = pots[:, 0, :mine].reshape(NY, NC, nq, own_rows).transpose(2, 0, 1, 3)
+    return targets, flat.reshape(-1)
 
 
 def solution(mesh):

time: 152 us -> 134 us (0.88)
  Pallas kernels: 147 us -> 129 us
    pallas_call x1, Pallas kernels: 147 us -> 129 us  [on_device(): pl.pallas_call(functools.partial(kernel, width * nd), out_shape=(jax.Shap...]
    unnamed x5 -> x1, local copies, waits for them, and re-layouts: 3.11 us -> 2.29 us
where the time goes in v2:
time: 134 us
  Pallas kernels  129 us (96%)
  local copies, waits for them, and re-layouts  3.78 us (3%)
    pallas_call x1, Pallas kernels, on_device(): pl.pallas_call(functools.partial(kernel, width * nd), out_shape=(jax.Shap...  129 us

profile of v2, /device:TPU:1, one launch (start us, length us, event | category | flops | bytes accessed | tf_op | source)
XLA Modules:
  0.0 133.9 jit_solution(17443600625772023293)
XLA Ops:
  0.6 129.4 %shard_map.41 = (bf16[128,4096]{1,0:T(8,128)(2,1)}, f32[8,1,256]{2,1,0:T(1,128)}) custom-call(bf16[128,4096]{1,0:T(8,128)(2,1)} %x_ref.1, bf16[24,4096]{1,0:T(8,128)(2,1)} %y_ref.1), custom_call_target="tpu_custom_call" | custom-call | tf_op jit(solution)/shard_map/pallas_call | solution.py:513
  130.1 0.7 slice_reduce_fusion
  130.8 0.1 reshape_squeeze.3
  130.9 0.7 reshape.7
  131.6 2.3 %copy.8 = bf16[128,4096]{1,0:T(8,128)(2,1)} copy(bf16[128,4096]{1,0:T(8,128)(2,1)} %get-tuple-element.8) | data formatting | bytes 2097152
  (1 shorter events, 0.0 us)

commit v3 on v2

--- a/solution.py
+++ b/solution.py
@@ -11,6 +11,7 @@
 ITERS = 3
 NZ, NX, NY, NC = 16, 4, 4, 2
 PIECES = 6
+SPLIT = 1
 LAG = 3
 NEG = -1e30
 MESH = pl.DeviceIdType.MESH
@@ -30,15 +31,17 @@
     dims_total, x_ref, y_ref, t_ref, pot_ref,
     ybuf, ysend, yr, xg, yg, x2, part, cx, sm, rs, a1, a2, pb, rbuf, zbuf, xbuf, pbuf, full, pall, wt, tst,
     y_s, y_r, x_s, x_r, own_sem, ring_s, ring_r, core_s, core_r, sum_s, sum_r,
-    row_s, row_r, cz_s, cz_r, cx_s, cx_r, pot_s, pot_r, one_s, one_r, set_s, set_r, core2_s, core2_r, t_s, t_r, to_sem,
+    row_s, row_r, cz_s, cz_r, cx_s, cx_r, pot_s, pot_r, one_s, one_r, set_s, set_r, core2_s, core2_r, t_s, t_r,
 ):
     rows_dev, width = x_ref.shape
     quarter = width // NX
     half = quarter // 2
     block_rows = NX * 24
     own_rows = block_rows // NC
-    nq = NZ // NY
-    mine = nq * own_rows
+    pairs = NY // SPLIT
+    nq = NZ // pairs
+    share = own_rows // SPLIT
+    mine = nq * share
     padded = a1.shape[0]
     piece = block_rows // PIECES
     columns = NZ * block_rows
@@ -94,15 +97,16 @@
         xt = lax.rem(x + o, NX)
         return copy(ysend.at[xt], yr.at[x], y_s.at[o - 1], y_r.at[o - 1], at(xt, y, z, c))
 
-    def x_copy(o):
+    x_piece = 16
+
+    def x_copy(o, k=None):
         xt = lax.rem(x + o, NX)
         cols = pl.ds(pl.multiple_of(xt * quarter, quarter), quarter)
-        return copy(x_ref.at[:, cols], xg.at[x], x_s.at[o - 1], x_r.at[o - 1], at(xt, y, z, c))
+        rows = pl.ds(0, rows_dev) if k is None else pl.ds(k * x_piece, x_piece)
+        return copy(x_ref.at[rows, cols], xg.at[x, rows], x_s.at[o - 1], x_r.at[o - 1], at(xt, y, z, c))
 
     for o in range(1, NX):
         y_copy(o).start()
-    for o in range(1, NX):
-        x_copy(o).start()
     own_x = pltpu.make_async_copy(
         x_ref.at[:, pl.ds(pl.multiple_of(x * quarter, quarter), quarter)], xg.at[x], own_sem.at[0]
     )
@@ -111,10 +115,7 @@
     for o in range(1, NX):
         y_copy(o).wait()
 
-    def slot(z_):
-        return lax.rem(z_, NY) * nq + z_ // NY
-
-    mid = slot(z)
+    mid = z
     pieces = []
     for k in range(NX):
         rows = yr[k].astype(F32)
@@ -122,31 +123,29 @@
         pieces.append(jnp.concatenate([rows[0:8, quarter:], rows[8:16, quarter:]], axis=1))
     yg[mid] = jnp.concatenate(pieces, axis=0).astype(BF16)
 
-    def ring_copy(way, step, u, z_):
-        rows = pl.ds(pl.multiple_of(u * piece, piece), piece)
-        ref = yg.at[slot(z_), rows]
-        to = lax.rem(z + 1, NZ) if way == 0 else lax.rem(z + NZ - 1, NZ)
-        return copy(ref, ref, ring_s.at[way, step - 1, u], ring_r.at[way, step - 1, u], at(x, y, to, c))
-
-    def origin(way, step):
-        return lax.rem(z + NZ - step, NZ) if way == 0 else lax.rem(z + step, NZ)
+    ahead = (at(x, y, lax.rem(z + 1, NZ), c), at(x, y, lax.rem(z + NZ - 1, NZ), c))
+
+    def ring_copy(way, step, u, place):
+        ref = yg.at[place, pl.ds(pl.multiple_of(u * piece, piece), piece)]
+        return copy(ref, ref, ring_s.at[way, step - 1, u], ring_r.at[way, step - 1, u], ahead[way])
+
+    def origins(step):
+        return lax.rem(z + NZ - step, NZ), lax.rem(z + step, NZ)
 
     last = NZ // 2
 
     def ring_first(u, _):
         for way in range(2):
-            ring_copy(way, 1, u, z).start()
+            ring_copy(way, 1, u, mid).start()
         return 0
 
     lax.fori_loop(0, PIECES, ring_first, 0)
 
-    def pass_on(step, u):
+    def pass_on(step, u, places, ways=(0, 1)):
         for way in range(2):
-            ring_copy(way, step, u, origin(way, step)).wait_recv()
-
-            @pl.when((step < last - 1) | ((u < PIECES // 2) == (way == 0)))
-            def _():
-                ring_copy(way, step + 1, u, origin(way, step)).start()
+            ring_copy(way, step, u, places[way]).wait_recv()
+            if way in ways:
+                ring_copy(way, step + 1, u, places[way]).start()
 
     def source(b):
         away = (b + 1) // 2
@@ -156,7 +155,7 @@
         return copy(part.at[s, other], cx.at[s], core_s.at[s], core_r.at[s], at(x, y, z, other))
 
     def distance(b):
-        s = slot(source(b))
+        s = source(b)
         rows = yg[s]
         noise_block = xg[...].reshape(NX * rows_dev, quarter)
         products = lax.dot_general(rows, noise_block, (((1,), (1,)), ((), ())), preferred_element_type=F32)
@@ -167,39 +166,39 @@
             part[s, k] = value[k * own_rows : (k + 1) * own_rows]
         core_copy(s).start()
 
-    def sum_copy(s, o, zs):
-        xt = lax.rem(x + o, NX)
+    def sum_copy(zs, o, h):
+        xt, q = lax.rem(x + o, NX), zs // pairs
         return copy(
-            sm.at[s, xt], rs.at[me_xy, zs // NY], sum_s.at[s, o], sum_r.at[me_xy, zs // NY],
-            at(xt, lax.rem(zs, NY), z, c),
+            sm.at[zs, xt, h], rs.at[me_xy, q], sum_s.at[zs, o, h], sum_r.at[me_xy, q],
+            at(xt, SPLIT * lax.rem(zs, pairs) + h, z, c),
         )
 
     def hand_out(b):
         zs = source(b)
-        s = slot(zs)
-        core_copy(s).wait()
-        value = part[s, c] + cx[s]
+        core_copy(zs).wait()
+        value = part[zs, c] + cx[zs]
         for k in range(NX):
-            sm[s, k] = value[:, k * rows_dev : (k + 1) * rows_dev]
+            for h in range(SPLIT):
+                sm[zs, k, h] = value[h * share : (h + 1) * share, k * rows_dev : (k + 1) * rows_dev]
         for o in range(1, NX):
-            sum_copy(s, o, zs).start()
-
-        @pl.when(lax.rem(zs, NY) == y)
-        def _():
-            rs[me_xy, zs // NY] = sm[s, x]
-
-        @pl.when(lax.rem(zs, NY) != y)
-        def _():
-            sum_copy(s, 0, zs).start()
-
-    def early(step, _):
-        def each(u, _):
-            pass_on(step, u)
-            return 0
-
-        return lax.fori_loop(0, PIECES, each, 0)
-
-    lax.fori_loop(1, LAG, early, 0)
+            for h in range(SPLIT):
+                sum_copy(zs, o, h).start()
+        for h in range(SPLIT):
+            @pl.when(SPLIT * lax.rem(zs, pairs) + h == y)
+            def _():
+                rs[me_xy, zs // pairs] = sm[zs, x, h]
+
+            @pl.when(SPLIT * lax.rem(zs, pairs) + h != y)
+            def _():
+                sum_copy(zs, 0, h).start()
+
+    x_turns = rows_dev // x_piece
+    for k in range(max(x_turns, (LAG - 1) * PIECES)):
+        if k < x_turns:
+            for o in range(1, NX):
+                x_copy(o, k).start()
+        if k < (LAG - 1) * PIECES:
+            pass_on(1 + k // PIECES, k % PIECES, origins(1 + k // PIECES))
 
     own_x.wait()
     for o in range(1, NX):
@@ -225,15 +224,22 @@
             hand_out(b - per)
 
     def later(step, _):
+        places = origins(step)
+
         def each(i, _):
-            pass_on(step, 2 * i)
-            pass_on(step, 2 * i + 1)
+            pass_on(step, 2 * i, places)
+            pass_on(step, 2 * i + 1, places)
             work(step, i)
             return 0
 
         return lax.fori_loop(0, per, each, 0)
 
-    lax.fori_loop(LAG, last, later, 0)
+    lax.fori_loop(LAG, last - 1, later, 0)
+    places = origins(last - 1)
+    for i in range(per):
+        for u in (2 * i, 2 * i + 1):
+            pass_on(last - 1, u, places, (0,) if u < PIECES // 2 else (1,))
+        work(last - 1, i)
     far = lax.rem(z + last, NZ)
 
     def ring_last(i, _):
@@ -254,48 +260,59 @@
         return 0
 
     lax.fori_loop(min(done, blocks), blocks, rest_distance, 0)
+    distance(NZ - 1)
     lax.fori_loop(max(min(done - per, blocks), 0), blocks, rest, 0)
-    distance(NZ - 1)
-
-    def ring_sent(step, _):
-        def each(u, _):
-            for way in range(2):
-                @pl.when((step < last) | ((u < PIECES // 2) == (way == 0)))
+    hand_out(NZ - 1)
+
+    def sum_up(b, _):
+        zs = source(b)
+
+        @pl.when(lax.rem(zs, pairs) == y // SPLIT)
+        def _():
+            q = zs // pairs
+
+            def arrive(src, _):
+                @pl.when(src != me_xy)
                 def _():
-                    ring_copy(way, step, u, z).wait_send()
+                    copy(rs.at[src, q], rs.at[src, q], sum_s.at[0, 0, 0], sum_r.at[src, q], here).wait_recv()
+
+                return 0
+
+            lax.fori_loop(0, NX * NY, arrive, 0)
+            total = rs[0, q]
+            for src in range(1, NX * NY):
+                total = total + rs[src, q]
+            a1[pl.ds(pl.multiple_of(q * share, 8), share), :] = total * (-1.0 / entropic)
+
+        return 0
+
+    lax.fori_loop(0, NZ, sum_up, 0)
+
+    def sent_so_far():
+        def ring_sent(step, _):
+            def each(u, _):
+                for way in range(2):
+                    @pl.when((step < last) | ((u < PIECES // 2) == (way == 0)))
+                    def _():
+                        ring_copy(way, step, u, mid).wait_send()
+                return 0
+
+            return lax.fori_loop(0, PIECES, each, 0)
+
+        def sums_sent(zs, _):
+            for h in range(SPLIT):
+                for o in range(1, NX):
+                    sum_copy(zs, o, h).wait_send()
+
+                @pl.when(SPLIT * lax.rem(zs, pairs) + h != y)
+                def _():
+                    sum_copy(zs, 0, h).wait_send()
+
             return 0
 
-        return lax.fori_loop(0, PIECES, each, 0)
-
-    lax.fori_loop(1, last + 1, ring_sent, 0)
-    hand_out(NZ - 1)
-
-    def sums_sent(zs, _):
-        for o in range(1, NX):
-            sum_copy(slot(zs), o, zs).wait_send()
-
-        @pl.when(lax.rem(zs, NY) != y)
-        def _():
-            sum_copy(slot(zs), 0, zs).wait_send()
-
-        return 0
-
-    lax.fori_loop(0, NZ, sums_sent, 0)
-
-    def sums_in(src, _):
-        @pl.when(src != me_xy)
-        def _():
-            for q in range(nq):
-                copy(rs.at[src, q], rs.at[src, q], sum_s.at[0, 0], sum_r.at[src, q], here).wait_recv()
-
-        return 0
-
-    lax.fori_loop(0, NX * NY, sums_in, 0)
-    for q in range(nq):
-        total = rs[0, q]
-        for src in range(1, NX * NY):
-            total = total + rs[src, q]
-        a1[q * own_rows : (q + 1) * own_rows, :] = total * (-1.0 / entropic)
+        lax.fori_loop(1, last + 1, ring_sent, 0)
+        lax.fori_loop(0, NZ, sums_sent, 0)
+
     if padded > mine:
         a1[mine:padded, :] = jnp.full((padded - mine, rows_dev), NEG, F32)
     for h in range(padded // rows_dev):
@@ -411,6 +428,8 @@
             @pl.when(it == k)
             def _():
                 by_core(part_of)
+                if k == 0:
+                    sent_so_far()
 
     real = lax.broadcasted_iota(jnp.int32, (1, padded), 1) < mine
 
@@ -441,7 +460,6 @@
         pot_s, pot_r, lambda: by_core(last_part),
     )
     pots = math.log(noise) - logsumexp0(found.reshape(NX, NY * NC, 1, padded))[0]
-    pot_ref[...] = pots * entropic
     for k in range(NY * NC):
         for h in range(padded // rows_dev):
             lo, hi = h * rows_dev, min((h + 1) * rows_dev, mine)
@@ -449,14 +467,10 @@
 
     by_core(all_in)
 
-    def t_copy(o):
+    def t_copy(o, h):
         xt = lax.rem(x + o, NX)
-        cols = pl.ds(pl.multiple_of(x * quarter, quarter), quarter)
-        return copy(tst.at[o], t_ref.at[:, cols], t_s.at[o], t_r.at[o], at(xt, y, z, c))
-
-    own_t = pltpu.make_async_copy(
-        tst.at[0], t_ref.at[:, pl.ds(pl.multiple_of(x * quarter, quarter), quarter)], to_sem.at[0]
-    )
+        cols = pl.ds(pl.multiple_of(x * quarter + h * half, half), half)
+        return copy(tst.at[o, h], t_ref.at[:, cols], t_s.at[o, h], t_r.at[o, h], at(xt, y, z, c))
 
     def target(i, _):
         o = lax.rem(NX // 2 + i, NX)
@@ -465,30 +479,39 @@
         top = jnp.max(jnp.max(scores, axis=0), axis=0, keepdims=True)
         powers = jnp.exp(scores - top)
         weights = powers * (1.0 / jnp.sum(jnp.sum(powers, axis=0), axis=0, keepdims=True))
-        for k in range(NY * NC):
-            wt[k % NY, :, k // NY] = weights[k].reshape(nq, own_rows, rows_dev).astype(BF16)
+        for k in range(NC):
+            for pair in range(pairs):
+                both = [weights[k * NY + SPLIT * pair + h].reshape(nq, share, rows_dev) for h in range(SPLIT)]
+                wt[:, pair, k] = jnp.concatenate(both, axis=1).astype(BF16)
         w = wt[...].reshape(columns, rows_dev)
-        value = lax.dot_general(
-            w, yg[...].reshape(columns, quarter), (((0,), (0,)), ((), ())), preferred_element_type=F32
-        )
-        tst[o] = value.astype(BF16)
-
-        @pl.when(o > 0)
-        def _():
-            t_copy(o).start()
-
-        @pl.when(o == 0)
-        def _():
-            own_t.start()
+        for h in range(2):
+            value = lax.dot_general(
+                w, yg[:, :, h * half : (h + 1) * half].reshape(columns, half), (((0,), (0,)), ((), ())),
+                preferred_element_type=F32,
+            ).astype(BF16)
+
+            @pl.when(o > 0)
+            def _():
+                tst[o, h] = value
+                t_copy(o, h).start()
+
+            @pl.when(o == 0)
+            def _():
+                t_ref[:, pl.ds(pl.multiple_of(x * quarter + h * half, half), half)] = value
 
         return 0
 
     lax.fori_loop(0, NX, target, 0)
 
+    ordered = [
+        pots[(SPLIT * pair + h) * NC + k, :, q * share : (q + 1) * share]
+        for q in range(nq) for pair in range(pairs) for k in range(NC) for h in range(SPLIT)
+    ]
+    pot_ref[...] = (jnp.concatenate(ordered, axis=1) * entropic).reshape(columns)
     by_core(all_out)
-    own_t.wait()
     for o in range(1, NX):
-        t_copy(o).wait()
+        for h in range(2):
+            t_copy(o, h).wait()
 
 
 def on_device(noise_latents, data_latents):
@@ -496,8 +519,10 @@
     quarter = width // NX
     block_rows = NX * 24
     own_rows = block_rows // NC
-    nq = NZ // NY
-    mine = nq * own_rows
+    pairs = NY // SPLIT
+    nq = NZ // pairs
+    share = own_rows // SPLIT
+    mine = nq * share
     padded = -(-mine // rows_dev) * rows_dev
     nd = NY * NC
     dma = pltpu.SemaphoreType.DMA
@@ -505,19 +530,19 @@
     longest = max(NX, NY)
     sems = [
         (NX - 1,), (NX - 1,), (NX - 1,), (NX - 1,), (2,),
-        (2, last, PIECES), (2, last, PIECES), (NZ,), (NZ,), (NZ, NX), (NX * NY, nq),
+        (2, last, PIECES), (2, last, PIECES), (NZ,), (NZ,), (NZ, NX, SPLIT), (NX * NY, nq),
         (ITERS, nd - 1), (ITERS, nd - 1), (ITERS, NZ - 1), (ITERS, NZ - 1), (ITERS - 1, NX - 1), (ITERS - 1, NX - 1),
         (1, NX * nd - 1), (1, NX * nd - 1),
-        (longest,), (longest,), (longest,), (longest,), (longest,), (longest,), (NX,), (NX,), (1,),
+        (longest,), (longest,), (longest,), (longest,), (longest,), (longest,), (NX, 2), (NX, 2),
     ]
     targets, pots = pl.pallas_call(
         functools.partial(kernel, width * nd),
         out_shape=(
-            jax.ShapeDtypeStruct((rows_dev, width), BF16),
-            jax.ShapeDtypeStruct((nd, 1, padded), F32),
+            pltpu.VMEM((rows_dev, width), BF16),
+            jax.ShapeDtypeStruct((NZ * block_rows,), F32),
         ),
         in_specs=[pl.BlockSpec(memory_space=pl.ANY)] * 2,
-        out_specs=(pl.BlockSpec(memory_space=pl.ANY), pl.BlockSpec(memory_space=pltpu.VMEM)),
+        out_specs=(pl.BlockSpec(memory_space=pltpu.VMEM),) * 2,
         scratch_shapes=[
             pltpu.VMEM(data_latents.shape, BF16),
             pltpu.VMEM((NX, 16, quarter * 3 // 2), BF16),
@@ -527,8 +552,8 @@
             pltpu.VMEM((8, NX * rows_dev), F32),
             pltpu.VMEM((NZ, NC, own_rows, NX * rows_dev), F32),
             pltpu.VMEM((NZ, own_rows, NX * rows_dev), F32),
-            pltpu.VMEM((NZ, NX, own_rows, rows_dev), F32),
-            pltpu.VMEM((NX * NY, nq, own_rows, rows_dev), F32),
+            pltpu.VMEM((NZ, NX, SPLIT, share, rows_dev), F32),
+            pltpu.VMEM((NX * NY, nq, share, rows_dev), F32),
             pltpu.VMEM((padded, rows_dev), F32),
             pltpu.VMEM((rows_dev, padded), F32),
             pltpu.VMEM((padded, rows_dev), F32),
@@ -538,16 +563,15 @@
             pltpu.VMEM((1, NX * nd, 1, padded), F32),
             pltpu.VMEM((NC, NX, NY, mine, rows_dev), F32),
             pltpu.VMEM((nd, mine, rows_dev), F32),
-            pltpu.VMEM((NY, nq, NC, own_rows, rows_dev), BF16),
-            pltpu.VMEM((NX, rows_dev, quarter), BF16),
+            pltpu.VMEM((nq, pairs, NC, own_rows, rows_dev), BF16),
+            pltpu.VMEM((NX, 2, rows_dev, quarter // 2), BF16),
         ]
         + [dma(shape) for shape in sems],
         compiler_params=pltpu.CompilerParams(
             collective_id=0, has_side_effects=True, vmem_limit_bytes=60 * 1024 * 1024
         ),
     )(noise_latents, data_latents)
-    flat = pots[:, 0, :mine].reshape(NY, NC, nq, own_rows).transpose(2, 0, 1, 3)
-    return targets, flat.reshape(-1)
+    return targets, pots
 
 
 def solution(mesh):

time: 134 us -> 130 us (0.970)
  local copies, waits for them, and re-layouts: 3.78 us -> 1.58 us
    pallas_call x1, Pallas kernels: 129 us -> 128 us  [on_device(): pl.pallas_call(functools.partial(kernel, width * nd), out_shape=(pltpu.VM...]
where the time goes in v3:
time: 130 us
  Pallas kernels  128 us (98%)
  local copies, waits for them, and re-layouts  1.58 us (1%)
    pallas_call x1, Pallas kernels, on_device(): pl.pallas_call(functools.partial(kernel, width * nd), out_shape=(pltpu.VM...  128 us

profile of v3, /device:TPU:1, one launch (start us, length us, event | category | flops | bytes accessed | tf_op | source)
XLA Modules:
  0.0 130.2 jit_solution(1296179748758996002)
XLA Ops:
  0.6 128.0 %shard_map.41 = (bf16[128,4096]{1,0:T(8,128)(2,1)S(1)}, f32[1536]{0:T(1024)}) custom-call(bf16[128,4096]{1,0:T(8,128)(2,1)} %x_ref.1, bf16[24,4096]{1,0:T(8,128)(2,1)} %y_ref.1), custom_call_target="tpu_custom_call" | custom-call | tf_op jit(solution)/shard_map/pallas_call | solution.py:538
  128.6 0.0 copy-start
  128.6 1.0 copy.6
  129.6 0.0 copy-done
  129.6 0.6 copy.7
Async XLA Ops:
  128.6 1.0 copy-start

commit v4 on v3

--- a/solution.py
+++ b/solution.py
@@ -12,6 +12,7 @@
 NZ, NX, NY, NC = 16, 4, 4, 2
 PIECES = 6
 SPLIT = 1
+UNROLL = 3
 LAG = 3
 NEG = -1e30
 MESH = pl.DeviceIdType.MESH
@@ -169,7 +170,7 @@
     def sum_copy(zs, o, h):
         xt, q = lax.rem(x + o, NX), zs // pairs
         return copy(
-            sm.at[zs, xt, h], rs.at[me_xy, q], sum_s.at[zs, o, h], sum_r.at[me_xy, q],
+            sm.at[zs, xt, h], rs.at[q, me_xy], sum_s.at[zs, o, h], sum_r.at[q],
             at(xt, SPLIT * lax.rem(zs, pairs) + h, z, c),
         )
 
@@ -186,7 +187,7 @@
         for h in range(SPLIT):
             @pl.when(SPLIT * lax.rem(zs, pairs) + h == y)
             def _():
-                rs[me_xy, zs // pairs] = sm[zs, x, h]
+                rs[zs // pairs, me_xy] = sm[zs, x, h]
 
             @pl.when(SPLIT * lax.rem(zs, pairs) + h != y)
             def _():
@@ -271,17 +272,11 @@
         def _():
             q = zs // pairs
 
-            def arrive(src, _):
-                @pl.when(src != me_xy)
-                def _():
-                    copy(rs.at[src, q], rs.at[src, q], sum_s.at[0, 0, 0], sum_r.at[src, q], here).wait_recv()
-
-                return 0
-
-            lax.fori_loop(0, NX * NY, arrive, 0)
-            total = rs[0, q]
+            others = rs.at[q, pl.ds(0, NX * NY - 1)]
+            copy(others, others, sum_s.at[0, 0, 0], sum_r.at[q], here).wait_recv()
+            total = rs[q, 0]
             for src in range(1, NX * NY):
-                total = total + rs[src, q]
+                total = total + rs[q, src]
             a1[pl.ds(pl.multiple_of(q * share, 8), share), :] = total * (-1.0 / entropic)
 
         return 0
@@ -321,25 +316,16 @@
     pb[...] = jnp.zeros_like(pb)
 
     def exchange(buf, it, me, n, peer, send, recv, beside=lambda: None):
-        def desc(i, who):
-            return copy(buf.at[it, who], buf.at[it, who], send.at[it, i - 1], recv.at[it, i - 1], peer(lax.rem(me + i, n)))
-
         def begin(i, _):
-            desc(i, me).start()
+            copy(buf.at[it, me], buf.at[it, me], send.at[it], recv.at[it], peer(lax.rem(me + i, n))).start()
             return 0
 
-        def sent(i, _):
-            desc(i, me).wait_send()
-            return 0
-
-        def end(i, _):
-            desc(i, lax.rem(me + n - i, n)).wait_recv()
-            return 0
-
-        lax.fori_loop(1, n, begin, 0)
+        lax.fori_loop(1, n, begin, 0, unroll=UNROLL)
         beside()
-        lax.fori_loop(1, n, sent, 0)
-        lax.fori_loop(1, n, end, 0)
+        others = buf.at[it, pl.ds(0, n - 1)]
+        whole = copy(others, others, send.at[it], recv.at[it], here)
+        whole.wait_recv()
+        whole.wait_send()
         return buf[it]
 
     def yc_peer(k):
@@ -433,18 +419,17 @@
 
     real = lax.broadcasted_iota(jnp.int32, (1, padded), 1) < mine
 
-    def columns_along_z(it):
+    def columns_here(it):
         row = spread(math.log(columns) - row_total(it), rows_dev)
-        for h in range(padded // rows_dev):
-            cut = slice(h * rows_dev, (h + 1) * rows_dev)
-            zbuf[it, z, :, cut] = logsumexp0(a2[:, cut] + row)
-        return logsumexp0(
-            exchange(zbuf, it, z, NZ, lambda k: at(x, y, k, c), cz_s, cz_r, lambda: spread_scores(it))
+        return jnp.concatenate(
+            [logsumexp0(a2[:, h : h + rows_dev] + row) for h in range(0, padded, rows_dev)], axis=1
+        )
+
+    def iteration(it, _):
+        zbuf[it, r_id] = columns_here(it)
+        total = logsumexp0(
+            exchange(zbuf, it, r_id, NZ * NX, lambda k: (k, d_id), cz_s, cz_r, lambda: spread_scores(it))
         )[0]
-
-    def iteration(it, _):
-        xbuf[it, x] = columns_along_z(it)
-        total = logsumexp0(exchange(xbuf, it, x, NX, lambda k: at(k, y, z, c), cx_s, cx_r))[0]
         p = jnp.where(real, math.log(noise) - total, 0.0)
         for h in range(padded // rows_dev):
             cut = slice(h * rows_dev, (h + 1) * rows_dev)
@@ -454,7 +439,12 @@
     lax.fori_loop(0, ITERS - 1, iteration, 0)
 
     me_plane = x * NY * NC + d_id
-    pbuf[0, me_plane] = columns_along_z(ITERS - 1)
+    xbuf[0, z] = columns_here(ITERS - 1)
+    pbuf[0, me_plane] = logsumexp0(
+        exchange(
+            xbuf, 0, z, NZ, lambda k: at(x, y, k, c), cx_s, cx_r, lambda: spread_scores(ITERS - 1)
+        )
+    )[0]
     found = exchange(
         pbuf, 0, me_plane, NX * NY * NC, lambda k: (z * NX + k // (NY * NC), lax.rem(k, NY * NC)),
         pot_s, pot_r, lambda: by_core(last_part),
@@ -530,9 +520,9 @@
     longest = max(NX, NY)
     sems = [
         (NX - 1,), (NX - 1,), (NX - 1,), (NX - 1,), (2,),
-        (2, last, PIECES), (2, last, PIECES), (NZ,), (NZ,), (NZ, NX, SPLIT), (NX * NY, nq),
-        (ITERS, nd - 1), (ITERS, nd - 1), (ITERS, NZ - 1), (ITERS, NZ - 1), (ITERS - 1, NX - 1), (ITERS - 1, NX - 1),
-        (1, NX * nd - 1), (1, NX * nd - 1),
+        (2, last, PIECES), (2, last, PIECES), (NZ,), (NZ,), (NZ, NX, SPLIT), (nq,),
+        (ITERS,), (ITERS,), (ITERS - 1,), (ITERS - 1,), (1,), (1,),
+        (1,), (1,),
         (longest,), (longest,), (longest,), (longest,), (longest,), (longest,), (NX, 2), (NX, 2),
     ]
     targets, pots = pl.pallas_call(
@@ -553,13 +543,13 @@
             pltpu.VMEM((NZ, NC, own_rows, NX * rows_dev), F32),
             pltpu.VMEM((NZ, own_rows, NX * rows_dev), F32),
             pltpu.VMEM((NZ, NX, SPLIT, share, rows_dev), F32),
-            pltpu.VMEM((NX * NY, nq, share, rows_dev), F32),
+            pltpu.VMEM((nq, NX * NY, share, rows_dev), F32),
             pltpu.VMEM((padded, rows_dev), F32),
             pltpu.VMEM((rows_dev, padded), F32),
             pltpu.VMEM((padded, rows_dev), F32),
             pltpu.VMEM((ITERS, nd, 1, rows_dev), F32),
-            pltpu.VMEM((ITERS, NZ, 1, padded), F32),
-            pltpu.VMEM((ITERS - 1, NX, 1, padded), F32),
+            pltpu.VMEM((ITERS - 1, NZ * NX, 1, padded), F32),
+            pltpu.VMEM((1, NZ, 1, padded), F32),
             pltpu.VMEM((1, NX * nd, 1, padded), F32),
             pltpu.VMEM((NC, NX, NY, mine, rows_dev), F32),
             pltpu.VMEM((nd, mine, rows_dev), F32),

time: 130 us -> 124 us (0.954)
  Pallas kernels: 128 us -> 122 us
    pallas_call x1, Pallas kernels: 128 us -> 122 us  [on_device(): pl.pallas_call(functools.partial(kernel, width * nd), out_shape=(pltpu.VM...]
where the time goes in v4:
time: 124 us
  Pallas kernels  122 us (98%)
  local copies, waits for them, and re-layouts  1.58 us (1%)
    pallas_call x1, Pallas kernels, on_device(): pl.pallas_call(functools.partial(kernel, width * nd), out_shape=(pltpu.VM...  122 us

profile of v4, /device:TPU:1, one launch (start us, length us, event | category | flops | bytes accessed | tf_op | source)
XLA Modules:
  0.0 124.3 jit_solution(5212660100341117631)
XLA Ops:
  0.6 122.1 %shard_map.41 = (bf16[128,4096]{1,0:T(8,128)(2,1)S(1)}, f32[1536]{0:T(1024)}) custom-call(bf16[128,4096]{1,0:T(8,128)(2,1)} %x_ref.1, bf16[24,4096]{1,0:T(8,128)(2,1)} %y_ref.1), custom_call_target="tpu_custom_call" | custom-call | tf_op jit(solution)/shard_map/pallas_call | solution.py:528
  122.7 0.0 copy-start
  122.7 1.0 copy.6
  123.7 0.0 copy-done
  123.7 0.6 copy.7
Async XLA Ops:
  122.7 1.0 copy-start

commit v5 on v4

--- a/solution.py
+++ b/solution.py
@@ -30,7 +30,7 @@
 
 def kernel(
     dims_total, x_ref, y_ref, t_ref, pot_ref,
-    ybuf, ysend, yr, xg, yg, x2, part, cx, sm, rs, a1, a2, pb, rbuf, zbuf, xbuf, pbuf, full, pall, wt, tst,
+    ysend, yr, xg, yg, x2, part, cx, sm, rs, a1, a2, pb, rbuf, zbuf, xbuf, pbuf, full, pall, wt, tst,
     y_s, y_r, x_s, x_r, own_sem, ring_s, ring_r, core_s, core_r, sum_s, sum_r,
     row_s, row_r, cz_s, cz_r, cx_s, cx_r, pot_s, pot_r, one_s, one_r, set_s, set_r, core2_s, core2_r, t_s, t_r,
 ):
@@ -68,9 +68,6 @@
     def xy_peer(o):
         return lax.rem(x + o // NY, NX), lax.rem(y + lax.rem(o, NY), NY)
 
-    fetch = pltpu.make_async_copy(y_ref, ybuf, own_sem.at[1])
-    fetch.start()
-
     barrier = pltpu.get_barrier_semaphore()
 
     def greet(to):
@@ -84,8 +81,7 @@
     greet(at(x, y, lax.rem(z + NZ - 1, NZ), c))
     greet(at(x, y, z, other))
 
-    fetch.wait()
-    wide = ybuf[...].astype(F32)
+    wide = y_ref[...].astype(F32)
     for q in range(NX):
         lo = wide[16:24, q * quarter : q * quarter + half]
         hi = wide[16:24, q * quarter + half : (q + 1) * quarter]
@@ -519,7 +515,7 @@
     last = NZ // 2
     longest = max(NX, NY)
     sems = [
-        (NX - 1,), (NX - 1,), (NX - 1,), (NX - 1,), (2,),
+        (NX - 1,), (NX - 1,), (NX - 1,), (NX - 1,), (1,),
         (2, last, PIECES), (2, last, PIECES), (NZ,), (NZ,), (NZ, NX, SPLIT), (nq,),
         (ITERS,), (ITERS,), (ITERS - 1,), (ITERS - 1,), (1,), (1,),
         (1,), (1,),
@@ -531,10 +527,9 @@
             pltpu.VMEM((rows_dev, width), BF16),
             jax.ShapeDtypeStruct((NZ * block_rows,), F32),
         ),
-        in_specs=[pl.BlockSpec(memory_space=pl.ANY)] * 2,
+        in_specs=[pl.BlockSpec(memory_space=pl.ANY), pl.BlockSpec(memory_space=pltpu.VMEM)],
         out_specs=(pl.BlockSpec(memory_space=pltpu.VMEM),) * 2,
         scratch_shapes=[
-            pltpu.VMEM(data_latents.shape, BF16),
             pltpu.VMEM((NX, 16, quarter * 3 // 2), BF16),
             pltpu.VMEM((NX, 16, quarter * 3 // 2), BF16),
             pltpu.VMEM((NX, rows_dev, quarter), BF16),

time: 124 us -> 126 us (1.016)
  Pallas kernels: 122 us -> 124 us
    pallas_call x1, Pallas kernels: 122 us -> 124 us  [on_device(): pl.pallas_call(functools.partial(kernel, width * nd), out_shape=(pltpu.VM...]
where the time goes in v5:
time: 126 us
  Pallas kernels  124 us (98%)
  local copies, waits for them, and re-layouts  1.58 us (1%)
    pallas_call x1, Pallas kernels, on_device(): pl.pallas_call(functools.partial(kernel, width * nd), out_shape=(pltpu.VM...  124 us

profile of v5, /device:TPU:1, one launch (start us, length us, event | category | flops | bytes accessed | tf_op | source)
XLA Modules:
  0.0 126.0 jit_solution(13548823735367023357)
XLA Ops:
  0.6 123.8 %shard_map.41 = (bf16[128,4096]{1,0:T(8,128)(2,1)S(1)}, f32[1536]{0:T(1024)}) custom-call(bf16[128,4096]{1,0:T(8,128)(2,1)} %x_ref.1, bf16[24,4096]{1,0:T(8,128)(2,1)} %y_ref.1), custom_call_target="tpu_custom_call" | custom-call | tf_op jit(solution)/shard_map/pallas_call | solution.py:524
  124.4 0.0 copy-start
  124.4 1.0 copy.6
  125.4 0.0 copy-done
  125.4 0.6 copy.7
Async XLA Ops:
  124.4 1.0 copy-start
